TPU v7x, 512 devices: a whole 4x8x8 slice. The times are simulated.
512 devices in a mesh: row: 64 (over y, z_hi, core), rep: 8 (over z_lo, x).
Axes of the slice: x: 4, y: 8, z: 8 (z_hi: 4, z_lo: 2; z = z_hi * 2 + z_lo), core: 2. Of those that a mesh axis runs over, the one named last changes fastest.
Arguments:
- features: bfloat16 [512, 128, 128], P(('row', 'rep')), may hold values from -6 to 6
- tile_values: bfloat16 [16384, 128, 128], P(('row', 'rep')), may hold values from -0.3125 to 0.3125
- tile_rows: int32 [16384], P(('row', 'rep')), may hold values from 0 to 511, as said below
- tile_cols: int32 [16384], P(('row', 'rep')), may hold values from 0 to 511, as said below
- tile_count: int32 [512], P(('row', 'rep')), may hold values from 8 to 32, as said below
- weights: bfloat16 [3, 128, 128], replicated, may hold values from -0.75 to 0.75
- biases: float32 [3, 128], replicated, may hold values from -3 to 3
Outputs:
- output: bfloat16 [512, 128, 128], P(('row', 'rep'))
Inputs may be any that keep to these rules, and one draw needn't show every extreme that they name: `tile_rows`: A slot of device d = r * 8 + c has its row block in r * 8 .. (r + 1) * 8 - 1. `tile_cols`: A slot of device d = r * 8 + c has a column block j with (j) % 8 == c; within a device the column blocks never fall from slot to slot. `tile_count`: some device has all of its slots live.
All inputs are finite; a program needn't handle non-finite values.
Results may differ from a plain program's by a relative error of at most 0.015.
Values may be sent and summed in bfloat16 or wider, within the bound.
A program may use at most 64 MiB of HBM per device.

v0:
```python
import jax
import jax.numpy as jnp
from jax import lax
from jax.sharding import PartitionSpec as P


def shards(features, tile_values, tile_rows, tile_cols, tile_count, weights, biases):
    rep_size = lax.axis_size("rep")
    block_count = features.shape[0]
    group_rows = rep_size * block_count
    slot_total = tile_values.shape[0]
    row_index = lax.axis_index("row")
    local_rows = tile_rows - row_index * group_rows
    col_local = tile_cols // block_count // rep_size * block_count + tile_cols % block_count
    live_count = tile_count[0]
    slot_ids = jnp.arange(slot_total, dtype=jnp.int32)
    alive_mask = slot_ids < live_count
    group_ids = jnp.arange(group_rows, dtype=jnp.int32)
    hidden = features
    for layer_idx in range(weights.shape[0]):
        panel_blocks = lax.all_gather(hidden, "row", axis=0, tiled=True)
        picked = jnp.take(panel_blocks, col_local, axis=0)
        product = jnp.einsum(
            "tij,tjf->tif", tile_values, picked, preferred_element_type=jnp.float32
        )
        select = ((local_rows[None, :] == group_ids[:, None]) & alive_mask[None, :]).astype(
            jnp.float32
        )
        partial_value = jnp.einsum("rt,tif->rif", select, product, precision=lax.Precision.HIGH)
        aggregate = lax.psum_scatter(partial_value, "rep", scatter_dimension=0, tiled=True).astype(
            jnp.bfloat16
        )
        mixed_rows = jnp.einsum(
            "bif,fg->big", aggregate, weights[layer_idx], preferred_element_type=jnp.float32
        )
        hidden = jnp.maximum(mixed_rows + biases[layer_idx], 0.0).astype(jnp.bfloat16)
    return hidden


def solution(mesh):
    in_specs = (
        P(("row", "rep"), None, None),
        P(("row", "rep"), None, None),
        P(("row", "rep")),
        P(("row", "rep")),
        P(("row", "rep")),
        P(),
        P(),
    )
    out_specs = P(("row", "rep"), None, None)
    return jax.shard_map(shards, mesh=mesh, in_specs=in_specs, out_specs=out_specs, check_vma=False)
```

profile of v0, /device:TPU:1, one launch (start us, length us, event | category | flops | bytes accessed | tf_op | source)
XLA Modules:
  0.0 428.8 jit_solution(5022474216587893826)
XLA Ops:
  6.5 0.0 copy-start
  6.5 0.0 all-gather.6.cloned.1.call-start
  6.5 0.7 all-gather.6.cloned.1.call-update
  7.3 0.0 reduce-scatter.4.cloned.1.call-start
  8.0 0.7 compare_and_fusion
  8.7 0.7 broadcast_subtract_fusion
  9.3 92.2 %all-gather.6.cloned.1.call-done = bf16[64,128,128]{2,1,0:T(8,128)(2,1)} async-done(((bf16[1,128,128]{2,1,0:T(8,128)(2,1)}), bf16[64,128,128]{2,1,0:T(8,128)(2,1)}) %all-gather.6.cloned.1.call-update) | async-done | bytes 2097168 | tf_op jit(solution)/shard_map/all_gather | solution.py:21
  101.5 3.2 gather_fusion
  104.7 0.0 copy-done
  104.7 2.2 convolution_bitcast_fusion.2
  107.0 2.1 copy.16
  109.0 0.0 copy-start.2
  109.0 0.0 copy-start.1
  109.0 2.1 fusion.34
  111.1 0.9 copy.17
  112.0 0.0 reduce-scatter.4.cloned.1.call-update
  112.0 0.0 all-gather.8.cloned.1.call-start
  112.1 0.0 copy-done.2
  112.1 34.9 %reduce-scatter.4.cloned.1.call-done = f32[1,128,128]{2,1,0:T(8,128)} async-done(((f32[8,128,128]{2,1,0:T(8,128)}), f32[1,128,128]{2,1,0:T(8,128)}) %reduce-scatter.4.cloned.1.call-update) | async-done | bytes 65552 | tf_op jit(solution)/shard_map/reduce_scatter | solution.py:30
  147.0 0.0 copy-done.1
  147.0 1.6 fusion.3
  148.6 0.0 all-gather.8.cloned.1.call-update
  148.6 0.0 reduce-scatter.6.cloned.1.call-start
  148.7 90.9 %all-gather.8.cloned.1.call-done = bf16[8192,128]{1,0:T(8,128)(2,1)} async-done(((bf16[128,128]{1,0:T(8,128)(2,1)}), bf16[8192,128]{1,0:T(8,128)(2,1)}) %all-gather.8.cloned.1.call-update) | async-done | bytes 2097168 | tf_op jit(solution)/shard_map/all_gather | solution.py:21
  239.6 3.2 gather_fusion.1
  242.8 2.2 convolution_bitcast_fusion.1
  245.0 2.1 copy.19
  247.1 2.0 fusion.32
  249.1 0.9 copy.20
  250.0 0.0 reduce-scatter.6.cloned.1.call-update
  250.1 0.0 all-gather.10.cloned.1.call-start
  250.1 35.0 %reduce-scatter.6.cloned.1.call-done = f32[1,128,128]{2,1,0:T(8,128)} async-done(((f32[8,128,128]{2,1,0:T(8,128)}), f32[1,128,128]{2,1,0:T(8,128)}) %reduce-scatter.6.cloned.1.call-update) | async-done | bytes 65552 | tf_op jit(solution)/shard_map/reduce_scatter | solution.py:30
  285.1 1.6 fusion.4
  286.7 0.0 all-gather.10.cloned.1.call-update
  286.7 0.0 reduce-scatter.8.cloned.1.call-start
  286.7 90.2 %all-gather.10.cloned.1.call-done = bf16[8192,128]{1,0:T(8,128)(2,1)} async-done(((bf16[128,128]{1,0:T(8,128)(2,1)}), bf16[8192,128]{1,0:T(8,128)(2,1)}) %all-gather.10.cloned.1.call-update) | async-done | bytes 2097168 | tf_op jit(solution)/shard_map/all_gather | solution.py:21
  376.9 2.3 gather_fusion.2
  379.3 2.3 convolution_bitcast_fusion
  381.6 2.4 copy.22
  384.0 0.5 fusion.30
  384.5 0.9 copy.23
  385.4 0.0 reduce-scatter.8.cloned.1.call-update
  385.4 35.0 %reduce-scatter.8.cloned.1.call-done = f32[1,128,128]{2,1,0:T(8,128)} async-done(((f32[8,128,128]{2,1,0:T(8,128)}), f32[1,128,128]{2,1,0:T(8,128)}) %reduce-scatter.8.cloned.1.call-update) | async-done | bytes 65552 | tf_op jit(solution)/shard_map/reduce_scatter | solution.py:30
  420.4 1.6 fusion.6
  (3 shorter events, 0.0 us)
Async XLA Ops:
  6.5 98.2 %copy-start = (bf16[32,128,128]{2,1,0:T(8,128)(2,1)S(1)}, bf16[32,128,128]{2,1,0:T(8,128)(2,1)}, u32[]{:S(2)}) copy-start(bf16[32,128,128]{2,1,0:T(8,128)(2,1)} %param.10) | copy-start | bytes 3145732
  6.5 95.0 %all-gather.6.cloned.1.call-start = ((), (), s32[]{:S(2)}) async-start(), calls=%async_computation.3 | async-start | bytes 2129920 | tf_op jit(solution)/shard_map/all_gather | solution.py:21
  7.3 139.7 %reduce-scatter.4.cloned.1.call-start = ((), (), s32[]{:S(2)}) async-start(), calls=%async_computation.4 | async-start | bytes 589824 | tf_op jit(solution)/shard_map/reduce_scatter | solution.py:30
  109.0 3.0 copy-start.2
  109.0 38.0 %copy-start.1 = (bf16[3,128,128]{2,1,0:T(8,128)(2,1)S(1)}, bf16[3,128,128]{2,1,0:T(8,128)(2,1)}, u32[]{:S(2)}) copy-start(bf16[3,128,128]{2,1,0:T(8,128)(2,1)} %param.14) | copy-start | bytes 294916
  112.0 127.6 %all-gather.8.cloned.1.call-start = ((), (), s32[]{:S(2)}) async-start(), calls=%async_computation.7 | async-start | bytes 2129920 | tf_op jit(solution)/shard_map/all_gather | solution.py:21
  148.6 136.5 %reduce-scatter.6.cloned.1.call-start = ((), (), s32[]{:S(2)}) async-start(), calls=%async_computation.5 | async-start | bytes 589824 | tf_op jit(solution)/shard_map/reduce_scatter | solution.py:30
  250.1 126.9 %all-gather.10.cloned.1.call-start = ((), (), s32[]{:S(2)}) async-start(), calls=%async_computation.8 | async-start | bytes 2129920 | tf_op jit(solution)/shard_map/all_gather | solution.py:21
  286.7 133.7 %reduce-scatter.8.cloned.1.call-start = ((), (), s32[]{:S(2)}) async-start(), calls=%async_computation.6 | async-start | bytes 589824 | tf_op jit(solution)/shard_map/reduce_scatter | solution.py:30
Sparse Core Ops, SparseCore 0:
  10.7 90.7 all-gather.5
  112.1 34.8 reduce-scatter.3
  150.8 88.7 all-gather.7
  250.2 34.8 reduce-scatter.5
  288.2 88.6 all-gather.9
  385.5 34.8 reduce-scatter.7
where the time goes:
time: 433 us; the launch traced here: 429 us
  waiting for transfers between devices  379 us (88%)
  local copies, waits for them, and re-layouts  18 us (4%)
  matrix products  16.1 us (4%)
  between operations  14.2 us (3%)
    all_gather x3, waiting for transfers between devices, shards(): panel_blocks = lax.all_gather(hidden, 'row', axis=0, tiled=True)  273 us
    reduce_scatter x3, waiting for transfers between devices, shards(): lax.psum_scatter(partial_value, 'rep', scatter_dimension=0, tiled=True)  105 us
    gather x3, local copies, waits for them, and re-layouts, shards(): picked = jnp.take(panel_blocks, col_local, axis=0)  8.81 us
  transfers between devices with their start and end apart: 6, of which 6 were waited for; matrix products, arithmetic and copies ran while one was open for 0% of the time, Pallas kernels for 0%

commit v1 on v0

v1 whole, which is shorter than its diff:
```python
import jax
import jax.numpy as jnp
from jax import lax
from jax.experimental import pallas as pl
from jax.experimental.pallas import tpu as pltpu
from jax.sharding import PartitionSpec as P

MESH = pl.DeviceIdType.MESH
NY, NZ, NC = 8, 4, 2
CUT = 64


def plan_kernel(rows_ref, cols_ref, count_ref, plan_ref, keep_ref, ends_ref, has_ref, fill):
    slots, groups = rows_ref.shape[0], ends_ref.shape[0]
    live = count_ref[0]

    def clear(g, _):
        fill[g] = 0
        return 0

    def count(t, _):
        g = lax.rem(rows_ref[t], groups)
        fill[g] = fill[g] + (t < live).astype(jnp.int32)
        return 0

    def offsets(g, start):
        size = fill[g]
        fill[g] = start
        ends_ref[g] = jnp.maximum(start + size - 1, 0)
        has_ref[g] = (size > 0).astype(jnp.float32)
        return start + size

    def blank(t, _):
        plan_ref[0, t] = 0
        plan_ref[1, t] = 0
        keep_ref[t] = 0.0
        return 0

    def place(t, _):
        @pl.when(t < live)
        def _():
            g = lax.rem(rows_ref[t], groups)
            at = fill[g]
            fill[g] = at + 1
            plan_ref[0, at] = t
            plan_ref[1, at] = cols_ref[t] // groups
            keep_ref[at] = jnp.where(has_ref[g] > 1.5, 1.0, 0.0)
            has_ref[g] = 2.0

        return 0

    def settle(g, _):
        has_ref[g] = jnp.minimum(has_ref[g], 1.0)
        return 0

    lax.fori_loop(0, groups, clear, 0)
    lax.fori_loop(0, slots, count, 0)
    lax.fori_loop(0, groups, offsets, 0)
    lax.fori_loop(0, slots, blank, 0)
    lax.fori_loop(0, slots, place, 0)
    lax.fori_loop(0, groups, settle, 0)


def layers_kernel(
    plan_ref, keep_ref, ends_ref, has_ref, feat_ref, tiles_hbm, weights_ref, biases_ref, out_ref,
    tiles, panel_0, panel_1, panel_2, runs, parts, inbox, hidden,
    tile_sem, z_out, z_in, y_out, y_in, a_out, a_in, b_out, b_in, s_out, s_in, r_out, r_in,
):
    slots = tiles.shape[0]
    reps = parts.shape[1]
    row, rep = lax.axis_index("row"), lax.axis_index("rep")
    core = lax.rem(row, NC)
    z = lax.rem(row // NC, NZ)
    y = row // (NC * NZ)

    def row_of(dy, dz, other=0):
        yy = lax.rem(y + dy + NY, NY)
        zz = lax.rem(z + dz + NZ, NZ)
        cc = 1 - core if other else core
        return (yy * NZ + zz) * NC + cc

    def at(dy, dz, other=0):
        return (row_of(dy, dz, other), rep)

    load = pltpu.make_async_copy(tiles_hbm, tiles, tile_sem)
    load.start()

    barrier = pltpu.get_barrier_semaphore()
    peers = [at(dy, 0) for dy in range(1, NY)] + [at(0, dz) for dz in range(1, NZ)] + [at(0, 0, 1)]
    peers += [(row, lax.rem(rep + k, reps)) for k in range(1, reps)]
    for peer in peers:
        pl.semaphore_signal(barrier, inc=1, device_id=peer, device_id_type=MESH)
    hidden[...] = feat_ref[0]
    pl.semaphore_wait(barrier, len(peers))

    def remote(src, dst, out_sem, in_sem, device):
        return pltpu.make_async_remote_copy(
            src_ref=src, dst_ref=dst, send_sem=out_sem, recv_sem=in_sem, device_id=device, device_id_type=MESH
        )

    def layer(l, panel):
        panel[row] = hidden[...]

        def z_copy(dz, src):
            ref = panel.at[src]
            return remote(ref, ref, z_out.at[l, dz - 1], z_in.at[l, dz - 1], at(0, dz))

        def y_copy(dy, src):
            ref = panel.at[src]
            return remote(ref, ref, y_out.at[l, dy - 1], y_in.at[l, dy - 1], at(dy, 0))

        def a_copy(dy, dz, src):
            ref = panel.at[src, pl.ds(0, CUT)]
            return remote(ref, ref, a_out.at[l, dz - 1, dy - 1], a_in.at[l, dz - 1, dy - 1], at(dy, 0))

        def b_copy(dy, dz, src):
            ref = panel.at[src, pl.ds(CUT, 128 - CUT)]
            return remote(ref, ref, b_out.at[l, dz - 1, dy - 1], b_in.at[l, dz - 1, dy - 1], at(0, dz))

        def s_copy(dy, dz, src):
            ref = panel.at[src]
            return remote(ref, ref, s_out.at[l, dz, dy], s_in.at[l, dz, dy], at(0, 0, 1))

        y_order = (1, 7, 2, 6, 3, 5, 4)
        z_order = (1, 3, 2)
        for k in range(7):
            y_copy(y_order[k], row).start()
            if k < 3:
                z_copy(z_order[k], row).start()
        s_copy(0, 0, row).start()
        for dz in z_order:
            src = row_of(0, -dz)
            z_copy(dz, src).wait_recv()
            for dy in y_order:
                a_copy(dy, dz, src).start()
            s_copy(0, dz, src).start()
        for dy in y_order:
            src = row_of(-dy, 0)
            y_copy(dy, src).wait_recv()
            for dz in z_order:
                b_copy(dy, dz, src).start()
            s_copy(dy, 0, src).start()
        for dz in z_order:
            for dy in y_order:
                src = row_of(-dy, -dz)
                a_copy(dy, dz, src).wait_recv()
                b_copy(dy, dz, src).wait_recv()
                s_copy(dy, dz, src).start()
        for dz in range(NZ):
            for dy in range(NY):
                s_copy(dy, dz, row_of(-dy, -dz, 1)).wait_recv()

        if l == 0:
            load.wait()

        def tile_step(p, acc):
            product = jnp.dot(
                tiles[plan_ref[0, p]], panel[plan_ref[1, p]], preferred_element_type=jnp.float32
            )
            acc = acc * keep_ref[p] + product
            runs[p] = acc
            return acc

        lax.fori_loop(0, slots, tile_step, jnp.zeros((128, 128), jnp.float32), unroll=4)

        def r_copy(k, dst):
            return remote(
                parts.at[l, k], inbox.at[l, k], r_out.at[l, k - 1], r_in.at[l, k - 1], (row, dst)
            )

        for k in range(1, reps):
            dst = lax.rem(rep + k, reps)
            parts[l, k] = (runs[ends_ref[dst]] * has_ref[dst]).astype(jnp.bfloat16)
            r_copy(k, dst).start()
        total = runs[ends_ref[rep]] * has_ref[rep]
        for k in range(1, reps):
            r_copy(k, rep).wait_recv()
            total += inbox[l, k].astype(jnp.float32)
        mixed = jnp.dot(
            total.astype(jnp.bfloat16), weights_ref[l], preferred_element_type=jnp.float32
        )
        hidden[...] = jnp.maximum(mixed + biases_ref[pl.ds(l, 1), :], 0.0).astype(jnp.bfloat16)

        for dz in range(1, NZ):
            z_copy(dz, row).wait_send()
        for dy in range(1, NY):
            y_copy(dy, row).wait_send()
        for dz in range(1, NZ):
            for dy in range(1, NY):
                a_copy(dy, dz, row).wait_send()
                b_copy(dy, dz, row).wait_send()
        for dz in range(NZ):
            for dy in range(NY):
                s_copy(dy, dz, row).wait_send()
        for k in range(1, reps):
            r_copy(k, rep).wait_send()

    for l, panel in enumerate((panel_0, panel_1, panel_2)):
        layer(l, panel)
    out_ref[0] = hidden[...]


def shards(features, tile_values, tile_rows, tile_cols, tile_count, weights, biases):
    slots = tile_values.shape[0]
    layers = weights.shape[0]
    reps = lax.axis_size("rep")
    smem = pl.BlockSpec(memory_space=pltpu.SMEM)
    vmem = pl.BlockSpec(memory_space=pltpu.VMEM)
    plan, keep, ends, has = pl.pallas_call(
        plan_kernel,
        out_shape=(
            jax.ShapeDtypeStruct((2, slots), jnp.int32),
            jax.ShapeDtypeStruct((slots,), jnp.float32),
            jax.ShapeDtypeStruct((reps,), jnp.int32),
            jax.ShapeDtypeStruct((reps,), jnp.float32),
        ),
        in_specs=[smem] * 3,
        out_specs=(smem,) * 4,
        scratch_shapes=[pltpu.SMEM((reps,), jnp.int32)],
        name="plan",
    )(tile_rows, tile_cols, tile_count)
    dma = pltpu.SemaphoreType.DMA
    return pl.pallas_call(
        layers_kernel,
        out_shape=jax.ShapeDtypeStruct(features.shape, jnp.bfloat16),
        in_specs=[smem] * 4 + [vmem, pl.BlockSpec(memory_space=pl.ANY), vmem, vmem],
        out_specs=vmem,
        scratch_shapes=[
            pltpu.VMEM((slots, 128, 128), jnp.bfloat16),
            pltpu.VMEM((NY * NZ * NC, 128, 128), jnp.bfloat16),
            pltpu.VMEM((NY * NZ * NC, 128, 128), jnp.bfloat16),
            pltpu.VMEM((NY * NZ * NC, 128, 128), jnp.bfloat16),
            pltpu.VMEM((slots, 128, 128), jnp.float32),
            pltpu.VMEM((layers, reps, 128, 128), jnp.bfloat16),
            pltpu.VMEM((layers, reps, 128, 128), jnp.bfloat16),
            pltpu.VMEM((128, 128), jnp.bfloat16),
            dma,
            dma((layers, NZ - 1)),
            dma((layers, NZ - 1)),
            dma((layers, NY - 1)),
            dma((layers, NY - 1)),
            dma((layers, NZ - 1, NY - 1)),
            dma((layers, NZ - 1, NY - 1)),
            dma((layers, NZ - 1, NY - 1)),
            dma((layers, NZ - 1, NY - 1)),
            dma((layers, NZ, NY)),
            dma((layers, NZ, NY)),
            dma((layers, reps - 1)),
            dma((layers, reps - 1)),
        ],
        compiler_params=pltpu.CompilerParams(
            collective_id=0, has_side_effects=True, vmem_limit_bytes=48 << 20
        ),
        name="layers",
    )(plan, keep, ends, has, features, tile_values, weights, biases)


def solution(mesh):
    in_specs = (
        P(("row", "rep"), None, None),
        P(("row", "rep"), None, None),
        P(("row", "rep")),
        P(("row", "rep")),
        P(("row", "rep")),
        P(),
        P(),
    )
    out_specs = P(("row", "rep"), None, None)
    return jax.shard_map(shards, mesh=mesh, in_specs=in_specs, out_specs=out_specs, check_vma=False)
```

time: 433 us -> 108 us (0.25)
  waiting for transfers between devices: 379 us -> 0 us
  Pallas kernels: 0 us -> 103 us
  matrix products: 16.1 us -> 0 us
  local copies, waits for them, and re-layouts: 18 us -> 4.17 us
  between operations: 14.2 us -> 0.71 us
    all_gather x3 -> x0, waiting for transfers between devices: 273 us -> none  [shards(): panel_blocks = lax.all_gather(hidden, 'row', axis=0, tiled=True)]
    reduce_scatter x3 -> x0, waiting for transfers between devices: 105 us -> none  [shards(): lax.psum_scatter(partial_value, 'rep', scatter_dimension=0, tiled=True)]
    pallas_call x0 -> x2, Pallas kernels: none -> 103 us  [the longest x1 100 us: shards(): pl.pallas_call(layers_kernel, out_shape=jax.ShapeDtypeStruct(features.sha...]
    dot_general x9 -> x0, matrix products: 16.1 us -> none  [the longest x3 6.77 us: shards(): jnp.einsum('tij,tjf->tif', tile_values, picked, preferred_element_type=jn...]
    dot_general x6 -> x0, local copies, waits for them, and re-layouts: 9.16 us -> none  [the longest x3 6.5 us: shards(): jnp.einsum('tij,tjf->tif', tile_values, picked, preferred_element_type=jn...]
    gather x3 -> x0, local copies, waits for them, and re-layouts: 8.81 us -> none  [shards(): picked = jnp.take(panel_blocks, col_local, axis=0)]
  transfers between devices with their start and end apart: 6 -> 0, of which waited for: 6 -> 0; matrix products, arithmetic and copies ran while one was open for 0% -> 0% of each run, Pallas kernels for 0% -> 0%
where the time goes in v1:
time: 108 us
  Pallas kernels  103 us (95%)
  local copies, waits for them, and re-layouts  4.17 us (4%)
    pallas_call x1, Pallas kernels, shards(): pl.pallas_call(layers_kernel, out_shape=jax.ShapeDtypeStruct(features.sha...  100 us
    unnamed x17, local copies, waits for them, and re-layouts  4.17 us
    pallas_call x1, Pallas kernels, shards(): pl.pallas_call(plan_kernel, out_shape=(jax.ShapeDtypeStruct((2, slots), j...  2.75 us

profile of v1, /device:TPU:1, one launch (start us, length us, event | category | flops | bytes accessed | tf_op | source)
XLA Modules:
  0.0 108.1 jit_solution(9043417843537735288)
XLA Ops:
  0.7 2.8 %plan.1 = (s32[2,32]{1,0:T(2,128)}, f32[32]{0:T(128)}, s32[8]{0:T(128)}, f32[8]{0:T(128)}) custom-call(s32[32]{0:T(128)} %rows_ref.1, s32[32]{0:T(128)} %cols_ref.1, s32[1]{0:T(128)S(6)} %copy.9.count_ref), custom_call_target="tpu_custom_call" | custom-call | tf_op jit(solution)/shard_map/plan/pallas_call | solution.py:209
  3.4 0.0 copy-start.6
  3.4 0.0 copy-start.7
  3.4 0.0 copy-start.3
  3.4 0.0 copy-start.4
  3.5 0.0 copy-start.5
  3.5 0.6 copy-done.6
  4.1 0.0 copy-done.7
  4.1 0.0 copy-done.3
  4.1 0.0 copy-done.4
  4.1 0.0 copy-done.5
  4.1 0.0 copy-start
  4.1 1.2 %copy-done = bf16[32,128,128]{2,1,0:T(8,128)(2,1)S(1)} copy-done((bf16[32,128,128]{2,1,0:T(8,128)(2,1)S(1)}, bf16[32,128,128]{2,1,0:T(8,128)(2,1)}, u32[]{:S(2)}) %copy-start) | copy-done | bytes 1048600
  5.4 0.0 copy-start.1
  5.4 0.9 copy-done.1
  6.3 0.0 copy-start.2
  6.3 0.8 copy-done.2
  7.0 100.4 %layers.1 = bf16[1,128,128]{2,1,0:T(8,128)(2,1)S(1)} custom-call(s32[2,32]{1,0:T(2,128)S(1)} %copy-done.4, f32[32]{0:T(128)S(1)} %copy-done.5, s32[8]{0:T(128)S(1)} %copy-done.6, f32[8]{0:T(128)S(1)} %copy-done.7, bf16[1,128,128]{2,1,0:T(8,128)(2,1)S(1)} %copy-done.2, bf16[32,128,128]{2,1,0:T(8,128)(2,1)S(1)} %copy-done, bf16[3,128,128]{2,1,0:T(8,128)(2,1)S(1)} %copy-done.1, ...), custom_call_target="tpu_custom_call" | custom-call | tf_op jit(solution)/shard_map/layers/pallas_call | solution.py:223
  107.5 0.6 copy.10
Async XLA Ops:
  3.4 0.7 copy-start.6
  3.4 0.6 copy-start.7
  3.4 0.7 copy-start.3
  3.4 0.7 copy-start.4
  3.5 0.7 copy-start.5
  4.1 1.2 %copy-start = (bf16[32,128,128]{2,1,0:T(8,128)(2,1)S(1)}, bf16[32,128,128]{2,1,0:T(8,128)(2,1)}, u32[]{:S(2)}) copy-start(bf16[32,128,128]{2,1,0:T(8,128)(2,1)} %tiles_hbm.1) | copy-start | bytes 3145732
  5.4 0.9 copy-start.1
  6.3 0.8 copy-start.2

commit v2 on v0

v2 whole, which is shorter than its diff:
```python
import jax
import jax.numpy as jnp
from jax import lax
from jax.experimental import pallas as pl
from jax.experimental.pallas import tpu as pltpu
from jax.sharding import PartitionSpec as P

MESH = pl.DeviceIdType.MESH
NY, NZ, NC = 8, 4, 2
GROUPS = 8
SIDE = 128
CUT = 80
HEAD = pl.ds(0, CUT)
TAIL = pl.ds(CUT, SIDE - CUT)


def layers_kernel(
    rows_hbm, cols_hbm, count_ref, feat_hbm, tiles_hbm, weights_hbm, biases_hbm, out_ref,
    rows, cols, before, ends, tiles, weights, biases, panel_0, panel_1, panel_2, runs, parts, inbox,
    load_sem, za_out, za_in, ya_out, ya_in, yb_out, yb_in, zb_out, zb_in,
    sa_out, sa_in, sb_out, sb_in, r_out, r_in,
):
    slots = tiles.shape[0]
    reps = parts.shape[1]
    row, rep = lax.axis_index("row"), lax.axis_index("rep")
    core = lax.rem(row, NC)
    z = lax.rem(row // NC, NZ)
    y = row // (NC * NZ)
    ys = [lax.rem(y + d, NY) for d in range(NY)]
    zs = [lax.rem(z + d, NZ) for d in range(NZ)]
    sibling = (row + 1 - 2 * core, rep)

    def y_peer(d):
        return ((ys[d] * NZ + z) * NC + core, rep)

    def z_peer(d):
        return ((y * NZ + zs[d]) * NC + core, rep)

    loads = [
        pltpu.make_async_copy(src, dst, load_sem.at[k])
        for k, (src, dst) in enumerate(
            (
                (feat_hbm.at[0], panel_0.at[core, y, z]),
                (rows_hbm, rows),
                (cols_hbm, cols),
                (tiles_hbm, tiles),
                (weights_hbm, weights),
                (biases_hbm, biases),
            )
        )
    ]
    for load in loads:
        load.start()

    barrier = pltpu.get_barrier_semaphore()
    peers = [y_peer(d) for d in range(1, NY)] + [z_peer(d) for d in range(1, NZ)] + [sibling]
    peers += [(row, lax.rem(rep + k, reps)) for k in range(1, reps)]
    for peer in peers:
        pl.semaphore_signal(barrier, inc=1, device_id=peer, device_id_type=MESH)
    loads[0].wait()
    pl.semaphore_wait(barrier, len(peers))

    def remote(src, dst, out_sem, in_sem, device):
        return pltpu.make_async_remote_copy(
            src_ref=src, dst_ref=dst, send_sem=out_sem, recv_sem=in_sem, device_id=device, device_id_type=MESH
        )

    def hop(d):
        return {3: 1, 5: 7}.get(d, d)

    def link_slots():
        for load in loads[1:3]:
            load.wait()
        live = count_ref[0]
        last = [jnp.int32(slots)] * GROUPS
        for t in range(slots):
            group = lax.rem(rows[t], GROUPS)
            previous = jnp.int32(slots)
            for g in range(GROUPS):
                hit = group == g
                previous = jnp.where(hit, last[g], previous)
                last[g] = jnp.where(hit & (t < live), t, last[g])
            before[t] = previous
        for g in range(GROUPS):
            ends[g] = last[g]

    def layer(l, panel):
        def za(d, src):
            ref = panel.at[core, y, src, HEAD]
            return remote(ref, ref, za_out.at[l, d], za_in.at[l, d], z_peer(d))

        def ya(d, src, part=0):
            if d == 4:
                ref = panel.at[core, src, pl.ds(2 * part, 2), HEAD]
                return remote(ref, ref, ya_out.at[l, NY * part + 4], ya_in.at[l, NY * part + 4], y_peer(6 if part else 2))
            ref = panel.at[core, src, :, HEAD]
            return remote(ref, ref, ya_out.at[l, d], ya_in.at[l, d], y_peer(hop(d)))

        def yb(d, src):
            ref = panel.at[core, src, z, TAIL]
            return remote(ref, ref, yb_out.at[l, d], yb_in.at[l, d], y_peer(2 if d == 4 else hop(d)))

        def zb(d, src):
            ref = panel.at[core, :, src, TAIL]
            return remote(ref, ref, zb_out.at[l, d], zb_in.at[l, d], z_peer(d))

        def sa(d, src, side):
            ref = panel.at[side, src, :, HEAD]
            return remote(ref, ref, sa_out.at[l, d], sa_in.at[l, d], sibling)

        def sb(d, src, side):
            ref = panel.at[side, :, src, TAIL]
            return remote(ref, ref, sb_out.at[l, d], sb_in.at[l, d], sibling)

        def back(d):
            return ys[(NY - d) % NY]

        def back_z(d):
            return zs[(NZ - d) % NZ]

        for d in (2, 6):
            yb(d, y).start()
        for d in (2, 1, 3):
            za(d, z).start()
        for d in (1, 7):
            yb(d, y).start()
        if l == 0:
            runs[...] = jnp.zeros_like(runs)
            link_slots()
        yb(2, back(2)).wait_recv()
        yb(4, back(2)).start()
        yb(3, back(2)).start()
        yb(6, back(6)).wait_recv()
        yb(5, back(6)).start()
        for d in (1, 3, 2):
            za(d, back_z(d)).wait_recv()
        for d in (2, 6, 1, 7):
            ya(d, y).start()
        sa(0, y, core).start()
        for d in (1, 7, 3, 5, 4):
            yb(d, back(d)).wait_recv()
        for d in (2, 1, 3):
            zb(d, z).start()
        sb(0, z, core).start()
        ya(2, back(2)).wait_recv()
        ya(4, back(2), 0).start()
        ya(3, back(2)).start()
        ya(6, back(6)).wait_recv()
        ya(4, back(6), 1).start()
        ya(5, back(6)).start()
        sa(2, back(2), core).start()
        sa(6, back(6), core).start()
        for d in (1, 7):
            ya(d, back(d)).wait_recv()
            sa(d, back(d), core).start()
        for d in (1, 3, 2):
            zb(d, back_z(d)).wait_recv()
            sb(d, back_z(d), core).start()
        for d in (3, 5):
            ya(d, back(d)).wait_recv()
            sa(d, back(d), core).start()
        for part in range(2):
            ya(4, back(4), part).wait_recv()
        sa(4, back(4), core).start()
        for d in range(NY):
            sa(d, back(d), 1 - core).wait_recv()
        for d in range(NZ):
            sb(d, back_z(d), 1 - core).wait_recv()

        if l == 0:
            for load in loads[3:]:
                load.wait()

        def tile_step(t, _):
            at = cols[t] // GROUPS
            block = panel[lax.rem(at, NC), at // (NC * NZ), lax.rem(at // NC, NZ)]
            product = jnp.dot(tiles[t], block, preferred_element_type=jnp.float32)
            runs[t] = runs[before[t]] + product
            return 0

        lax.fori_loop(0, slots, tile_step, 0, unroll=4)

        def r_copy(k, dst):
            return remote(
                parts.at[l, k], inbox.at[l, k], r_out.at[l, k], r_in.at[l, k], (row, dst)
            )

        for k in range(1, reps):
            dst = lax.rem(rep + k, reps)
            parts[l, k] = runs[ends[dst]].astype(jnp.bfloat16)
            r_copy(k, dst).start()
        for d in range(1, NY):
            yb(d, y).wait_send()
            if d != 4:
                ya(d, y).wait_send()
        for part in range(2):
            ya(4, y, part).wait_send()
        for d in range(1, NZ):
            za(d, z).wait_send()
            zb(d, z).wait_send()
        for d in range(NY):
            sa(d, y, core).wait_send()
        for d in range(NZ):
            sb(d, z, core).wait_send()
        total = runs[ends[rep]]
        for k in range(1, reps):
            r_copy(k, rep).wait_recv()
            total += inbox[l, k].astype(jnp.float32)
        mixed = jnp.dot(
            total.astype(jnp.bfloat16), weights[l], preferred_element_type=jnp.float32
        )
        return jnp.maximum(mixed + biases[pl.ds(l, 1), :], 0.0).astype(jnp.bfloat16)

    panels = (panel_0, panel_1, panel_2)
    for l, panel in enumerate(panels):
        result = layer(l, panel)
        if l + 1 < len(panels):
            panels[l + 1][core, y, z] = result
        else:
            out_ref[0] = result
    for l in range(len(panels)):
        for k in range(1, reps):
            remote(parts.at[l, k], inbox.at[l, k], r_out.at[l, k], r_in.at[l, k], sibling).wait_send()


def shards(features, tile_values, tile_rows, tile_cols, tile_count, weights, biases):
    slots = tile_values.shape[0]
    layers = weights.shape[0]
    reps = lax.axis_size("rep")
    smem = pl.BlockSpec(memory_space=pltpu.SMEM)
    hbm = pl.BlockSpec(memory_space=pl.ANY)
    dma = pltpu.SemaphoreType.DMA
    panel = pltpu.VMEM((NC, NY, NZ, SIDE, SIDE), jnp.bfloat16)
    return pl.pallas_call(
        layers_kernel,
        out_shape=jax.ShapeDtypeStruct(features.shape, jnp.bfloat16),
        in_specs=[hbm, hbm, smem, hbm, hbm, hbm, hbm],
        out_specs=pl.BlockSpec(memory_space=pltpu.VMEM),
        scratch_shapes=[
            pltpu.SMEM((slots,), jnp.int32),
            pltpu.SMEM((slots,), jnp.int32),
            pltpu.SMEM((slots,), jnp.int32),
            pltpu.SMEM((GROUPS,), jnp.int32),
            pltpu.VMEM((slots, SIDE, SIDE), jnp.bfloat16),
            pltpu.VMEM(weights.shape, jnp.bfloat16),
            pltpu.VMEM(biases.shape, jnp.float32),
            panel,
            panel,
            panel,
            pltpu.VMEM((slots + 1, SIDE, SIDE), jnp.float32),
            pltpu.VMEM((layers, reps, SIDE, SIDE), jnp.bfloat16),
            pltpu.VMEM((layers, reps, SIDE, SIDE), jnp.bfloat16),
            dma((6,)),
            dma((layers, NZ)),
            dma((layers, NZ)),
            dma((layers, 2 * NY)),
            dma((layers, 2 * NY)),
            dma((layers, NY)),
            dma((layers, NY)),
            dma((layers, NZ)),
            dma((layers, NZ)),
            dma((layers, NY)),
            dma((layers, NY)),
            dma((layers, NZ)),
            dma((layers, NZ)),
            dma((layers, reps)),
            dma((layers, reps)),
        ],
        compiler_params=pltpu.CompilerParams(
            collective_id=0, has_side_effects=True, vmem_limit_bytes=62 << 20
        ),
        name="layers",
    )(tile_rows, tile_cols, tile_count, features, tile_values, weights, biases)


def solution(mesh):
    in_specs = (
        P(("row", "rep"), None, None),
        P(("row", "rep"), None, None),
        P(("row", "rep")),
        P(("row", "rep")),
        P(("row", "rep")),
        P(),
        P(),
    )
    out_specs = P(("row", "rep"), None, None)
    return jax.shard_map(shards, mesh=mesh, in_specs=in_specs, out_specs=out_specs, check_vma=False)
```

time: 433 us -> 96.6 us (0.22)
  waiting for transfers between devices: 379 us -> 0 us
  Pallas kernels: 0 us -> 94.4 us
  local copies, waits for them, and re-layouts: 18 us -> 1.38 us
  matrix products: 16.1 us -> 0 us
  between operations: 14.2 us -> 0.66 us
    all_gather x3 -> x0, waiting for transfers between devices: 273 us -> none  [shards(): panel_blocks = lax.all_gather(hidden, 'row', axis=0, tiled=True)]
    reduce_scatter x3 -> x0, waiting for transfers between devices: 105 us -> none  [shards(): lax.psum_scatter(partial_value, 'rep', scatter_dimension=0, tiled=True)]
    pallas_call x0 -> x1, Pallas kernels: none -> 94.4 us  [shards(): pl.pallas_call(layers_kernel, out_shape=jax.ShapeDtypeStruct(features.sha...]
    dot_general x9 -> x0, matrix products: 16.1 us -> none  [the longest x3 6.77 us: shards(): jnp.einsum('tij,tjf->tif', tile_values, picked, preferred_element_type=jn...]
    dot_general x6 -> x0, local copies, waits for them, and re-layouts: 9.16 us -> none  [the longest x3 6.5 us: shards(): jnp.einsum('tij,tjf->tif', tile_values, picked, preferred_element_type=jn...]
    gather x3 -> x0, local copies, waits for them, and re-layouts: 8.81 us -> none  [shards(): picked = jnp.take(panel_blocks, col_local, axis=0)]
  transfers between devices with their start and end apart: 6 -> 0, of which waited for: 6 -> 0; matrix products, arithmetic and copies ran while one was open for 0% -> 0% of each run, Pallas kernels for 0% -> 0%
where the time goes in v2:
time: 96.6 us; the launch traced here: 96.4 us
  Pallas kernels  94.4 us (98%)
  local copies, waits for them, and re-layouts  1.38 us (1%)
    pallas_call x1, Pallas kernels, shards(): pl.pallas_call(layers_kernel, out_shape=jax.ShapeDtypeStruct(features.sha...  94.4 us

profile of v2, /device:TPU:1, one launch (start us, length us, event | category | flops | bytes accessed | tf_op | source)
XLA Modules:
  0.0 96.4 jit_solution(15125218377105060985)
XLA Ops:
  0.7 94.4 %layers.1 = bf16[1,128,128]{2,1,0:T(8,128)(2,1)} custom-call(s32[32]{0:T(128)} %rows_hbm.1, s32[32]{0:T(128)} %cols_hbm.1, s32[1]{0:T(128)S(6)} %copy.9.count_ref, bf16[1,128,128]{2,1,0:T(8,128)(2,1)} %feat_hbm.1, bf16[32,128,128]{2,1,0:T(8,128)(2,1)} %tiles_hbm.1, bf16[3,128,128]{2,1,0:T(8,128)(2,1)} %weights_hbm.1, f32[3,128]{1,0:T(4,128)} %biases_hbm.1), custom_call_target="tpu_custom_call" | custom-call | tf_op jit(solution)/shard_map/layers/pallas_call | solution.py:234
  95.0 1.4 %copy.10 = bf16[1,128,128]{2,1,0:T(8,128)(2,1)} copy(bf16[1,128,128]{2,1,0:T(8,128)(2,1)} %layers.1) | data formatting | bytes 65536

commit v3 on v2

v3 whole, which is shorter than its diff:
```python
import jax
import jax.numpy as jnp
from jax import lax
from jax.experimental import pallas as pl
from jax.experimental.pallas import tpu as pltpu
from jax.sharding import PartitionSpec as P

MESH = pl.DeviceIdType.MESH
NY, NZ, NC = 8, 4, 2
GROUPS = 8
SIDE = 128
ROWS = (pl.ds(0, SIDE),)
ALONG_Y = {(1, 1), (1, 2), (1, 3), (7, 1), (7, 2), (7, 3), (2, 2), (6, 2), (3, 2), (5, 2), (4, 2)}
OWN_ORDER = (
    ("y", 1), ("y", 7), ("z", 1), ("z", 3), ("y", 2), ("y", 6), ("z", 2), ("y", 3), ("y", 5), ("y", 4)
)
ARRIVAL_ORDER = (
    ("z", 1), ("z", 3), ("y", 1), ("y", 7), ("y", 2), ("y", 6), ("z", 2), ("y", 3), ("y", 5), ("y", 4)
)
LAST_ORDER = (
    (1, 1), (7, 1), (1, 3), (7, 3), (2, 1), (2, 3), (6, 1), (6, 3), (1, 2), (7, 2), (2, 2), (6, 2),
    (3, 1), (3, 3), (5, 1), (5, 3), (3, 2), (5, 2), (4, 1), (4, 3), (4, 2)
)


def layers_kernel(
    rows_hbm, cols_hbm, count_ref, feat_hbm, tiles_hbm, weights_hbm, biases_hbm, out_ref,
    rows, cols, place, before, ends, tiles, weights, biases, panel_0, panel_1, panel_2, runs, parts, inbox,
    load_sem, zo_out, zo_in, yo_out, yo_in, on_out, on_in, so_out, so_in, s_out, s_in, r_out, r_in,
):
    slots = tiles.shape[0]
    reps = parts.shape[1]
    panels = (panel_0, panel_1, panel_2)
    row, rep = lax.axis_index("row"), lax.axis_index("rep")
    core = lax.rem(row, NC)
    z = lax.rem(row // NC, NZ)
    y = row // (NC * NZ)
    ys = [lax.rem(y + d, NY) for d in range(NY)]
    zs = [lax.rem(z + d, NZ) for d in range(NZ)]
    sibling = (row + 1 - 2 * core, rep)

    def y_peer(d):
        return ((ys[d] * NZ + z) * NC + core, rep)

    def z_peer(d):
        return ((y * NZ + zs[d]) * NC + core, rep)

    loads = [
        pltpu.make_async_copy(src, dst, load_sem.at[k])
        for k, (src, dst) in enumerate(
            (
                (feat_hbm.at[0], panel_0.at[core, y, z]),
                (rows_hbm, rows),
                (cols_hbm, cols),
                (tiles_hbm, tiles),
                (weights_hbm, weights),
                (biases_hbm, biases),
            )
        )
    ]
    for load in loads:
        load.start()

    barrier = pltpu.get_barrier_semaphore()
    peers = [y_peer(d) for d in range(1, NY)] + [z_peer(d) for d in range(1, NZ)] + [sibling]
    peers += [(row, lax.rem(rep + k, reps)) for k in range(1, reps)]
    for peer in peers:
        pl.semaphore_signal(barrier, inc=1, device_id=peer, device_id_type=MESH)
    loads[0].wait()
    pl.semaphore_wait(barrier, len(peers))

    def remote(src, dst, out_sem, in_sem, device):
        return pltpu.make_async_remote_copy(
            src_ref=src, dst_ref=dst, send_sem=out_sem, recv_sem=in_sem, device_id=device, device_id_type=MESH
        )

    def link_slots():
        for load in loads[1:3]:
            load.wait()
        live = count_ref[0]
        last = [jnp.int32(slots)] * GROUPS
        for t in range(slots):
            group = lax.rem(rows[t], GROUPS)
            previous = jnp.int32(slots)
            for g in range(GROUPS):
                hit = group == g
                previous = jnp.where(hit, last[g], previous)
                last[g] = jnp.where(hit & (t < live), t, last[g])
            before[t] = previous
            at = cols[t] // GROUPS
            place[0, t] = lax.rem(at, NC)
            place[1, t] = at // (NC * NZ)
            place[2, t] = lax.rem(at // NC, NZ)
        for g in range(GROUPS):
            ends[g] = last[g]

    def back(d):
        return ys[(NY - d) % NY]

    def back_z(d):
        return zs[(NZ - d) % NZ]

    def zo(l, h, d, src):
        ref = panels[l].at[core, y, src, ROWS[h]]
        return remote(ref, ref, zo_out.at[l, h, d], zo_in.at[l, h, d], z_peer(d))

    def yo(l, h, d, src):
        ref = panels[l].at[core, src, z, ROWS[h]]
        return remote(ref, ref, yo_out.at[l, h, d], yo_in.at[l, h, d], y_peer(d))

    def so(l, h, side):
        ref = panels[l].at[side, y, z, ROWS[h]]
        return remote(ref, ref, so_out.at[l, h], so_in.at[l, h], sibling)

    def on(l, h, d, src, dz, src_z):
        ref = panels[l].at[core, src, src_z, ROWS[h]]
        peer = y_peer(d) if (d, dz) in ALONG_Y else z_peer(dz)
        return remote(ref, ref, on_out.at[l, h, dz, d], on_in.at[l, h, dz, d], peer)

    def sib(l, d, src, dz, src_z, side):
        ref = panels[l].at[side, src, src_z]
        return remote(ref, ref, s_out.at[l, dz, d], s_in.at[l, dz, d], sibling)

    def part(l, k, dst):
        src, to = parts.at[l, k], inbox.at[l, k]
        return remote(src, to, r_out.at[l, k], r_in.at[l, k], (row, dst))

    def send_own(l, h):
        for axis, d in OWN_ORDER:
            (yo(l, h, d, y) if axis == "y" else zo(l, h, d, z)).start()
        so(l, h, core).start()

    def gather(l):
        def y_arrival(d, h):
            yo(l, h, d, back(d)).wait_recv()
            for dz in (2, 1, 3):
                if (d, dz) not in ALONG_Y:
                    on(l, h, d, back(d), dz, z).start()
            if h == len(ROWS) - 1:
                sib(l, d, back(d), 0, z, core).start()

        def z_arrival(dz, h):
            zo(l, h, dz, back_z(dz)).wait_recv()
            for d in (4, 3, 5, 2, 6, 1, 7):
                if (d, dz) in ALONG_Y:
                    on(l, h, d, y, dz, back_z(dz)).start()
            if h == len(ROWS) - 1:
                sib(l, 0, y, dz, back_z(dz), core).start()

        for h in range(len(ROWS)):
            for axis, d in ARRIVAL_ORDER:
                (y_arrival if axis == "y" else z_arrival)(d, h)
        for d, dz in LAST_ORDER:
            for h in range(len(ROWS)):
                on(l, h, d, back(d), dz, back_z(dz)).wait_recv()
            sib(l, d, back(d), dz, back_z(dz), core).start()
        for h in range(len(ROWS)):
            so(l, h, 1 - core).wait_recv()
        for dz in range(NZ):
            for d in range(NY):
                if d or dz:
                    sib(l, d, back(d), dz, back_z(dz), 1 - core).wait_recv()

    def gather_sent(l):
        for h in range(len(ROWS)):
            so(l, h, core).wait_send()
            for d in range(1, NY):
                yo(l, h, d, y).wait_send()
            for dz in range(1, NZ):
                zo(l, h, dz, z).wait_send()
        for dz in range(NZ):
            for d in range(NY):
                if d and dz:
                    for h in range(len(ROWS)):
                        on(l, h, d, y, dz, z).wait_send()
                if d or dz:
                    sib(l, d, y, dz, z, core).wait_send()

    def products(l):
        def tile_step(t, _):
            block = panels[l][place[0, t], place[1, t], place[2, t]]
            product = jnp.dot(tiles[t], block, preferred_element_type=jnp.float32)
            runs[t] = runs[before[t]] + product
            return 0

        lax.fori_loop(0, slots, tile_step, 0, unroll=16)
        for k in range(1, reps):
            dst = lax.rem(rep + k, reps)
            parts[l, k] = runs[ends[dst]].astype(jnp.bfloat16)
            part(l, k, dst).start()

    def mix(l):
        total = runs[ends[rep]]
        for k in range(1, reps):
            part(l, k, rep).wait_recv()
            total += inbox[l, k].astype(jnp.float32)
        mixed = jnp.dot(
            total.astype(jnp.bfloat16), weights[l], preferred_element_type=jnp.float32
        )
        return jnp.maximum(mixed + biases[pl.ds(l, 1), :], 0.0).astype(jnp.bfloat16)

    layers = len(panels)
    for h in range(len(ROWS)):
        send_own(0, h)
    runs[...] = jnp.zeros_like(runs)
    link_slots()
    for l in range(layers):
        gather(l)
        if l == 0:
            for load in loads[3:]:
                load.wait()
        products(l)
        gather_sent(l)
        result = mix(l)
        if l + 1 < layers:
            panels[l + 1][core, y, z] = result
            for h in range(len(ROWS)):
                send_own(l + 1, h)
        else:
            out_ref[0] = result
    for l in range(layers):
        for k in range(1, reps):
            part(l, k, rep).wait_send()


def shards(features, tile_values, tile_rows, tile_cols, tile_count, weights, biases):
    slots = tile_values.shape[0]
    layers = weights.shape[0]
    reps = lax.axis_size("rep")
    smem = pl.BlockSpec(memory_space=pltpu.SMEM)
    hbm = pl.BlockSpec(memory_space=pl.ANY)
    dma = pltpu.SemaphoreType.DMA
    panel = pltpu.VMEM((NC, NY, NZ, SIDE, SIDE), jnp.bfloat16)
    return pl.pallas_call(
        layers_kernel,
        out_shape=jax.ShapeDtypeStruct(features.shape, jnp.bfloat16),
        in_specs=[hbm, hbm, smem, hbm, hbm, hbm, hbm],
        out_specs=pl.BlockSpec(memory_space=pltpu.VMEM),
        scratch_shapes=[
            pltpu.SMEM((slots,), jnp.int32),
            pltpu.SMEM((slots,), jnp.int32),
            pltpu.SMEM((3, slots), jnp.int32),
            pltpu.SMEM((slots,), jnp.int32),
            pltpu.SMEM((GROUPS,), jnp.int32),
            pltpu.VMEM((slots, SIDE, SIDE), jnp.bfloat16),
            pltpu.VMEM(weights.shape, jnp.bfloat16),
            pltpu.VMEM(biases.shape, jnp.float32),
            panel,
            panel,
            panel,
            pltpu.VMEM((slots + 1, SIDE, SIDE), jnp.float32),
            pltpu.VMEM((layers, reps, SIDE, SIDE), jnp.bfloat16),
            pltpu.VMEM((layers, reps, SIDE, SIDE), jnp.bfloat16),
            dma((6,)),
            dma((layers, len(ROWS), NZ)),
            dma((layers, len(ROWS), NZ)),
            dma((layers, len(ROWS), NY)),
            dma((layers, len(ROWS), NY)),
            dma((layers, len(ROWS), NZ, NY)),
            dma((layers, len(ROWS), NZ, NY)),
            dma((layers, len(ROWS))),
            dma((layers, len(ROWS))),
            dma((layers, NZ, NY)),
            dma((layers, NZ, NY)),
            dma((layers, reps)),
            dma((layers, reps)),
        ],
        compiler_params=pltpu.CompilerParams(
            collective_id=0, has_side_effects=True, vmem_limit_bytes=62 << 20
        ),
        name="layers",
    )(tile_rows, tile_cols, tile_count, features, tile_values, weights, biases)


def solution(mesh):
    in_specs = (
        P(("row", "rep"), None, None),
        P(("row", "rep"), None, None),
        P(("row", "rep")),
        P(("row", "rep")),
        P(("row", "rep")),
        P(),
        P(),
    )
    out_specs = P(("row", "rep"), None, None)
    return jax.shard_map(shards, mesh=mesh, in_specs=in_specs, out_specs=out_specs, check_vma=False)
```

time: 96.6 us -> 90.4 us (0.936)
  Pallas kernels: 94.4 us -> 88.2 us
    pallas_call x1, Pallas kernels: 94.4 us -> 88.2 us  [shards(): pl.pallas_call(layers_kernel, out_shape=jax.ShapeDtypeStruct(features.sha...]
where the time goes in v3:
time: 90.4 us; the launch traced here: 90.2 us
  Pallas kernels  88.2 us (98%)
  local copies, waits for them, and re-layouts  1.38 us (2%)
    pallas_call x1, Pallas kernels, shards(): pl.pallas_call(layers_kernel, out_shape=jax.ShapeDtypeStruct(features.sha...  88.2 us

profile of v3, /device:TPU:1, one launch (start us, length us, event | category | flops | bytes accessed | tf_op | source)
XLA Modules:
  0.0 90.2 jit_solution(5517319897815211358)
XLA Ops:
  0.7 88.2 %layers.1 = bf16[1,128,128]{2,1,0:T(8,128)(2,1)} custom-call(s32[32]{0:T(128)} %rows_hbm.1, s32[32]{0:T(128)} %cols_hbm.1, s32[1]{0:T(128)S(6)} %copy.9.count_ref, bf16[1,128,128]{2,1,0:T(8,128)(2,1)} %feat_hbm.1, bf16[32,128,128]{2,1,0:T(8,128)(2,1)} %tiles_hbm.1, bf16[3,128,128]{2,1,0:T(8,128)(2,1)} %weights_hbm.1, f32[3,128]{1,0:T(4,128)} %biases_hbm.1), custom_call_target="tpu_custom_call" | custom-call | tf_op jit(solution)/shard_map/layers/pallas_call | solution.py:234
  88.8 1.4 %copy.10 = bf16[1,128,128]{2,1,0:T(8,128)(2,1)} copy(bf16[1,128,128]{2,1,0:T(8,128)(2,1)} %layers.1) | data formatting | bytes 65536

commit v4 on v3

--- a/solution.py
+++ b/solution.py
@@ -133,7 +133,7 @@
     def gather(l):
         def y_arrival(d, h):
             yo(l, h, d, back(d)).wait_recv()
-            for dz in (2, 1, 3):
+            for dz in (1, 3, 2):
                 if (d, dz) not in ALONG_Y:
                     on(l, h, d, back(d), dz, z).start()
             if h == len(ROWS) - 1:
@@ -141,7 +141,7 @@
 
         def z_arrival(dz, h):
             zo(l, h, dz, back_z(dz)).wait_recv()
-            for d in (4, 3, 5, 2, 6, 1, 7):
+            for d in (1, 7, 2, 6, 3, 5, 4):
                 if (d, dz) in ALONG_Y:
                     on(l, h, d, y, dz, back_z(dz)).start()
             if h == len(ROWS) - 1:

time: 90.4 us -> 92.5 us (1.023)
  Pallas kernels: 88.2 us -> 90.2 us
    pallas_call x1, Pallas kernels: 88.2 us -> 90.2 us  [shards(): pl.pallas_call(layers_kernel, out_shape=jax.ShapeDtypeStruct(features.sha...]
where the time goes in v4:
time: 92.5 us; the launch traced here: 92.3 us
  Pallas kernels  90.2 us (98%)
  local copies, waits for them, and re-layouts  1.38 us (1%)
    pallas_call x1, Pallas kernels, shards(): pl.pallas_call(layers_kernel, out_shape=jax.ShapeDtypeStruct(features.sha...  90.2 us

profile of v4, /device:TPU:1, one launch (start us, length us, event | category | flops | bytes accessed | tf_op | source)
XLA Modules:
  0.0 92.3 jit_solution(6981413233559270951)
XLA Ops:
  0.7 90.2 %layers.1 = bf16[1,128,128]{2,1,0:T(8,128)(2,1)} custom-call(s32[32]{0:T(128)} %rows_hbm.1, s32[32]{0:T(128)} %cols_hbm.1, s32[1]{0:T(128)S(6)} %copy.9.count_ref, bf16[1,128,128]{2,1,0:T(8,128)(2,1)} %feat_hbm.1, bf16[32,128,128]{2,1,0:T(8,128)(2,1)} %tiles_hbm.1, bf16[3,128,128]{2,1,0:T(8,128)(2,1)} %weights_hbm.1, f32[3,128]{1,0:T(4,128)} %biases_hbm.1), custom_call_target="tpu_custom_call" | custom-call | tf_op jit(solution)/shard_map/layers/pallas_call | solution.py:234
  90.9 1.4 %copy.10 = bf16[1,128,128]{2,1,0:T(8,128)(2,1)} copy(bf16[1,128,128]{2,1,0:T(8,128)(2,1)} %layers.1) | data formatting | bytes 65536

commit v5 on v3

--- a/solution.py
+++ b/solution.py
@@ -183,7 +183,7 @@
             runs[t] = runs[before[t]] + product
             return 0
 
-        lax.fori_loop(0, slots, tile_step, 0, unroll=16)
+        lax.fori_loop(0, slots, tile_step, 0, unroll=32)
         for k in range(1, reps):
             dst = lax.rem(rep + k, reps)
             parts[l, k] = runs[ends[dst]].astype(jnp.bfloat16)

time: 90.4 us -> 90.2 us (level)
  no operation moved by 1% of the time
where the time goes in v5:
time: 90.2 us; the launch traced here: 90 us
  Pallas kernels  88 us (98%)
  local copies, waits for them, and re-layouts  1.38 us (2%)
    pallas_call x1, Pallas kernels, shards(): pl.pallas_call(layers_kernel, out_shape=jax.ShapeDtypeStruct(features.sha...  88 us

profile of v5, /device:TPU:1, one launch (start us, length us, event | category | flops | bytes accessed | tf_op | source)
XLA Modules:
  0.0 90.0 jit_solution(9665577562872592582)
XLA Ops:
  0.7 88.0 %layers.1 = bf16[1,128,128]{2,1,0:T(8,128)(2,1)} custom-call(s32[32]{0:T(128)} %rows_hbm.1, s32[32]{0:T(128)} %cols_hbm.1, s32[1]{0:T(128)S(6)} %copy.9.count_ref, bf16[1,128,128]{2,1,0:T(8,128)(2,1)} %feat_hbm.1, bf16[32,128,128]{2,1,0:T(8,128)(2,1)} %tiles_hbm.1, bf16[3,128,128]{2,1,0:T(8,128)(2,1)} %weights_hbm.1, f32[3,128]{1,0:T(4,128)} %biases_hbm.1), custom_call_target="tpu_custom_call" | custom-call | tf_op jit(solution)/shard_map/layers/pallas_call | solution.py:234
  88.6 1.4 %copy.10 = bf16[1,128,128]{2,1,0:T(8,128)(2,1)} copy(bf16[1,128,128]{2,1,0:T(8,128)(2,1)} %layers.1) | data formatting | bytes 65536
